TPU v7x, 32 devices: a whole 2x2x4 slice. The times are simulated.
32 devices in a mesh: groups: 2 (over x), owners: 16 (over z, y, core).
Axes of the slice: x: 2, y: 2, z: 4, core: 2. Of those that a mesh axis runs over, the one named last changes fastest.
Arguments:
- embeddings: bfloat16 [65536, 1536], P(('groups', 'owners')), parts along dimension 0, may hold values from -40 to 40
- level_ids: int32 [65536], P(('groups', 'owners')), parts along dimension 0, may hold values from 0 to 63, as said below
- centroids: float32 [2048, 1536], P(('groups', 'owners')), parts along dimension 0, may hold values from -8 to 8
- empty_ids: int32 [32], P('groups'), parts along dimension 0, may hold values from 0 to 1023, as said below
- reseed_rows: int32 [32], P('groups'), parts along dimension 0, may hold values from 0 to 32767
Outputs:
- new_centroids: float32 [2048, 1536], P(('groups', 'owners')), parts along dimension 0
- counts: float32 [2048], P(('groups', 'owners')), parts along dimension 0
There are 2 independent parts, one for each index of `groups`. A program takes and returns all parts, laid end to end along the dimension named above; each array names one. Nothing has to cross between parts.
Inputs may be any that keep to these rules, and one draw needn't show every extreme that they name: `level_ids`: From the rows of one owner at most 256 go to any one owner; in every draw some owner receives exactly 256 rows from every owner. `empty_ids`: the ids are distinct.
All inputs are finite; a program needn't handle non-finite values.
Results may differ from a plain program's by a relative error of at most 0.0075.
Values may be sent and summed in bfloat16 or wider, within the bound.
A program may use at most 128 MiB of HBM per device.

v0:
```python
import math

import jax
import jax.numpy as jnp
from jax import lax
from jax.sharding import PartitionSpec as P

L1_DEV = 4


PRIOR = 8.0


def group_softmax(logits, in_group):
    masked = jnp.where(in_group, logits, -1e30)
    column_peak = jnp.max(masked, axis=0, keepdims=True)
    raised = jnp.where(in_group, jnp.exp(masked - column_peak), 0.0)
    denominator = jnp.sum(raised, axis=0, keepdims=True)
    return raised / jnp.where(denominator > 0.0, denominator, 1.0)


def weigh(centroid_b, row_block, group_ids, row_groups):
    wide = centroid_b.astype(jnp.float32)
    norms_sq = jnp.sum(wide * wide, axis=1)
    scores = lax.dot_general(
        centroid_b, row_block, (((1,), (1,)), ((), ())), preferred_element_type=jnp.float32
    )
    logits = (scores - 0.5 * norms_sq[:, None]) / math.sqrt(row_block.shape[1])
    in_group = group_ids[:, None] == row_groups[None, :]
    weights = group_softmax(logits, in_group)
    weights_b = weights.astype(jnp.bfloat16)
    totals = jnp.dot(weights_b, row_block, preferred_element_type=jnp.float32)
    counts = jnp.sum(weights, axis=1)
    return (totals, counts)


def shards(embeddings, level_ids, centroids, empty_ids, reseed_rows):
    row_count, width = embeddings.shape
    position = lax.axis_index("owners")
    local_count = centroids.shape[0]
    per_group = local_count // L1_DEV
    centroid_b = centroids.astype(jnp.bfloat16)
    every_centroid = lax.all_gather(centroid_b, "owners", axis=0, tiled=True)
    group_ids = jnp.arange(every_centroid.shape[0], dtype=jnp.int32) // per_group
    local_totals, local_counts = weigh(every_centroid, embeddings, group_ids, level_ids)
    totals, counts = (
        lax.psum_scatter(local_totals, "owners", scatter_dimension=0, tiled=True),
        lax.psum_scatter(local_counts, "owners", scatter_dimension=0, tiled=True),
    )
    local_pick = reseed_rows - position * row_count
    present = (local_pick >= 0) & (local_pick < row_count)
    picked = embeddings[jnp.clip(local_pick, 0, row_count - 1)].astype(jnp.float32)
    picked = jnp.where(present[:, None], picked, 0.0)
    reseeds = lax.psum(picked.astype(jnp.bfloat16), "owners").astype(jnp.float32)
    updated = (totals + PRIOR * centroids) / (counts + PRIOR)[:, None]
    my_ids = position * local_count + jnp.arange(local_count, dtype=jnp.int32)
    selector = (empty_ids[:, None] == my_ids[None, :]).astype(jnp.float32)
    replaced = jnp.sum(selector, axis=0) > 0.0
    values = jnp.dot(
        selector.T, reseeds, precision=lax.Precision.HIGHEST, preferred_element_type=jnp.float32
    )
    new_centroids = jnp.where(replaced[:, None], values, updated)
    return (new_centroids, counts)


def solution(mesh):
    in_specs = (
        P(("groups", "owners"), None),
        P(("groups", "owners")),
        P(("groups", "owners"), None),
        P("groups"),
        P("groups"),
    )
    out_specs = (P(("groups", "owners"), None), P(("groups", "owners")))
    return jax.shard_map(shards, mesh=mesh, in_specs=in_specs, out_specs=out_specs, check_vma=False)
```

profile of v0, /device:TPU:0, one launch (start us, length us, event | category | flops | bytes accessed | tf_op | source)
XLA Modules:
  0.0 196.5 jit_solution(10748430002371543329)
XLA Ops:
  7.2 0.0 all-gather.2.cloned.1.call-start
  7.2 1.7 convert_element_type.22
  8.9 0.0 all-gather.2.cloned.1.call-update
  8.9 0.0 reduce-scatter.2.cloned.1.call-start
  9.0 49.8 %all-gather.2.cloned.1.call-done = bf16[1024,1536]{1,0:T(8,128)(2,1)} async-done(((bf16[64,1536]{1,0:T(8,128)(2,1)}), bf16[1024,1536]{1,0:T(8,128)(2,1)}) %all-gather.2.cloned.1.call-update) | async-done | bytes 3145744 | tf_op jit(solution)/shard_map/all_gather | solution.py:43
  58.8 2.6 %multiply_reduce_fusion = f32[1024]{0:T(1024)S(1)} fusion(bf16[1024,1536]{1,0:T(8,128)(2,1)} %all-gather.2.cloned.1.call-done), kind=kLoop, calls=%fused_computation.4 | loop fusion | flops 4717568 | bytes 3149824 | tf_op jit(solution)/shard_map/reduce_sum | solution.py:24
  61.4 0.0 slice-start
  61.4 0.0 copy-start.2
  61.4 0.0 slice-start.1
  61.4 10.2 %fusion = (f32[2048]{0:T(1024)S(1)}, f32[1024,2048]{1,0:T(8,128)S(1)}) fusion(f32[1024]{0:T(1024)S(1)} %broadcast_multiply_fusion, s32[2048]{0:T(1024)} %param.6, s32[1024]{0:T(1024)S(1)} %add_select_fusion, bf16[1024,1536]{1,0:T(8,128)(2,1)} %all-gather.2.cloned.1.call-done, bf16[2048,1536]{1,0:T(8,128)(2,1)} %param.5), kind=kOutput, calls=%fused_computation.3 | convolution fusion | flops 6452934656 | bytes 17850368 | tf_op jit(solution)/shard_map/dot_general | solution.py:25
  71.7 0.0 copy-start
  71.7 0.0 copy-done.2
  71.7 3.1 %fusion.2 = f32[2048]{0:T(1024)S(1)} fusion(f32[1024,2048]{1,0:T(8,128)S(1)} %get-tuple-element.5, f32[2048]{0:T(1024)S(1)} %get-tuple-element.4, f32[1024]{0:T(1024)S(1)} %broadcast_multiply_fusion, s32[2048]{0:T(1024)S(1)} %copy-done.2, s32[1024]{0:T(1024)S(1)} %add_select_fusion), kind=kLoop, calls=%fused_computation.6 | loop fusion | flops 14678016 | bytes 8421376 | tf_op jit(solution)/shard_map/reduce_sum | solution.py:18
  74.7 0.1 copy-done
  74.9 0.0 slice-done
  74.9 0.0 slice-done.1
  74.9 0.0 copy-start.5
  74.9 0.0 copy-start.4
  74.9 9.7 %fusion.3 = f32[1024,1536]{1,0:T(8,128)} fusion(bf16[2048,1536]{1,0:T(8,128)(2,1)S(1)} %bitcast.6, f32[1024,2048]{1,0:T(8,128)S(1)} %get-tuple-element.5, f32[2048]{0:T(1024)S(1)} %compare_select_fusion.2, f32[2048]{0:T(1024)S(1)} %get-tuple-element.4, f32[1024]{0:T(1024)S(1)} %broadcast_multiply_fusion, s32[2048]{0:T(1024)S(1)} %copy-done.2, ...), kind=kOutput, calls=%fused_computation.7 | convolution fusion | flops 6459228160 | bytes 21004288 | tf_op jit(solution)/shard_map/dot_general | solution.py:32
  84.6 0.0 reduce-scatter.2.cloned.1.call-update
  84.6 0.0 copy-done.3
  84.6 4.3 %gather_fusion = bf16[16,1536]{1,0:T(8,128)(2,1)S(1)} fusion(bf16[2048,1536]{1,0:T(8,128)(2,1)} %param.5, s32[1024]{0:T(1024)S(1)} %pad_clamp_fusion), kind=kCustom, calls=%fused_computation | custom fusion | bytes 98368 | tf_op jit(solution)/shard_map/gather | solution.py:52
  88.9 0.0 copy-done.5
  88.9 0.6 dynamic-slice
  90.2 0.1 select_convert_fusion
  90.3 61.2 %psum.7 = bf16[16,1536]{1,0:T(8,128)(2,1)S(1)} all-reduce(bf16[16,1536]{1,0:T(8,128)(2,1)S(1)} %select_convert_fusion), channel_id=1, replica_groups=mesh['groups'=2,'owners'=16] {'owners'}, use_global_device_ids=true, to_apply=%region_1.2 | all-reduce | flops 24576 | bytes 98304 | tf_op jit(solution)/shard_map/psum | solution.py:54
  151.5 0.0 copy-done.4
  151.5 0.1 fusion.6
  151.6 5.7 %fusion.12 = f32[1024]{0:T(1024)S(1)} fusion(f32[2048]{0:T(1024)S(1)} %compare_select_fusion.2, f32[2048]{0:T(1024)S(1)} %get-tuple-element.4, f32[1024,2048]{1,0:T(8,128)} %copy-done, f32[1024]{0:T(1024)S(1)} %broadcast_multiply_fusion, s32[2048]{0:T(1024)S(1)} %copy-done.2, s32[1024]{0:T(1024)S(1)} %add_select_fusion), kind=kLoop, calls=%fused_computation.31 | loop fusion | flops 16776192 | bytes 8425472 | tf_op jit(solution)/shard_map/reduce_sum | solution.py:33
  157.2 29.8 %all-reduce = f32[1024]{0:T(1024)S(1)} all-reduce(f32[1024]{0:T(1024)S(1)} %fusion.12), channel_id=3, replica_groups=mesh['groups'=2,'owners'=16] {'owners'}, use_global_device_ids=true, to_apply=%region_7.8.clone | all-reduce | flops 1024 | bytes 8192
  187.0 0.6 broadcast_add_fusion
  187.6 2.1 %convolution_select_fusion = f32[64,1536]{1,0:T(8,128)} fusion(bf16[16,1536]{1,0:T(8,128)(2,1)S(1)} %psum.7, f32[64,1536]{1,0:T(8,128)} %reduce-scatter.2.cloned.1.call-done, f32[64,1536]{1,0:T(8,128)S(1)} %copy-done.1, f32[64]{0:T(128)S(1)} %get-tuple-element.2, pred[64]{0:T(512)(128)(4,1)S(1)} %broadcast_compare_fusion, s32[64]{0:T(128)S(1)} %iota_add_fusion, ...), kind=kOutput, calls=%fused_computation.9 | convolution fusion | flops 3539968 | bytes 1229440 | tf_op jit(solution)/shard_map/dot_general | solution.py:59
  (13 shorter events, 0.1 us)
Async XLA Ops:
  7.2 51.6 %all-gather.2.cloned.1.call-start = ((), (), s32[]{:S(2)}) async-start(), calls=%async_computation.1 | async-start | bytes 3342336 | tf_op jit(solution)/shard_map/all_gather | solution.py:43
  8.9 178.7 %reduce-scatter.2.cloned.1.call-start = ((), (), s32[]{:S(2)}) async-start(), calls=%async_computation.2 | async-start | bytes 6684672 | tf_op jit(solution)/shard_map/reduce_scatter | solution.py:47
  61.4 13.5 %slice-start = ((s8[6291456]{0:T(1024)(128)(4,1)}), s8[4194304]{0:T(1024)(128)(4,1)S(1)}, s32[]{:S(2)}) async-start(s8[6291456]{0:T(1024)(128)(4,1)} %bitcast.5), calls=%async_computation.3 | async-start | bytes 8388608
  61.4 10.3 %copy-start.2 = (s32[2048]{0:T(1024)S(1)}, s32[2048]{0:T(1024)}, u32[]{:S(2)}) copy-start(s32[2048]{0:T(1024)} %param.6) | copy-start | bytes 24580
  61.4 13.5 %slice-start.1 = ((s8[6291456]{0:T(1024)(128)(4,1)}), s8[2097152]{0:T(1024)(128)(4,1)S(1)}, s32[]{:S(2)}) async-start(s8[6291456]{0:T(1024)(128)(4,1)} %bitcast.5), calls=%async_computation.4 | async-start | bytes 4194304
  71.7 3.2 %copy-start = (f32[1024,2048]{1,0:T(8,128)}, f32[1024,2048]{1,0:T(8,128)S(1)}, u32[]{:S(2)}) copy-start(f32[1024,2048]{1,0:T(8,128)S(1)} %get-tuple-element.5) | copy-start | bytes 25165828
  74.9 9.7 %copy-start.3 = (s32[16]{0:T(128)S(1)}, s32[16]{0:T(128)}, u32[]{:S(2)}) copy-start(s32[16]{0:T(128)} %param.9) | copy-start | bytes 196
  74.9 14.0 %copy-start.5 = (u32[32]{0:T(128)S(1)}, u32[32]{0:T(128)}, u32[]{:S(2)}) copy-start(u32[32]{0:T(128)} %constant.51) | copy-start | bytes 388
  74.9 76.6 %copy-start.4 = (s32[16]{0:T(128)S(1)}, s32[16]{0:T(128)}, u32[]{:S(2)}) copy-start(s32[16]{0:T(128)} %param.8) | copy-start | bytes 196
  84.6 103.0 %copy-start.1 = (f32[64,1536]{1,0:T(8,128)S(1)}, f32[64,1536]{1,0:T(8,128)}, u32[]{:S(2)}) copy-start(f32[64,1536]{1,0:T(8,128)} %param.7) | copy-start | bytes 1179652
Sparse Core Ops, SparseCore 0:
  10.9 47.8 all-gather.1
  84.7 84.7 reduce-scatter.1
where the time goes:
time: 197 us; the launch traced here: 196 us
  blocking collectives  91 us (46%)
  waiting for transfers between devices  49.8 us (25%)
  matrix products  22 us (11%)
  between operations  14.9 us (8%)
  other arithmetic  13.8 us (7%)
  local copies, waits for them, and re-layouts  5.02 us (3%)
    psum x1, blocking collectives, shards(): lax.psum(picked.astype(jnp.bfloat16), 'owners').astype(jnp.float32)  61.2 us
    all_gather x1, waiting for transfers between devices, shards(): every_centroid = lax.all_gather(centroid_b, 'owners', axis=0, tiled=True)  49.8 us
    unnamed x1, blocking collectives  29.8 us
    dot_general x1, matrix products, weigh(): lax.dot_general(centroid_b, row_block, (((1,), (1,)), ((), ())), preferre...  10.2 us
    dot_general x1, matrix products, weigh(): totals = jnp.dot(weights_b, row_block, preferred_element_type=jnp.float32)  9.66 us
    reduce_sum x1, other arithmetic, weigh(): counts = jnp.sum(weights, axis=1)  5.66 us
    gather x1, local copies, waits for them, and re-layouts, shards(): embeddings[jnp.clip(local_pick, 0, row_count - 1)].astype(jnp.float32)  4.27 us
  transfers between devices with their start and end apart: 2, of which 1 were waited for; matrix products, arithmetic and copies ran while one was open for 6% of the time, Pallas kernels for 0%

commit v1 on v0

v1 whole, which is shorter than its diff:
```python
import functools
import math

import jax
import jax.numpy as jnp
from jax import lax
from jax.experimental import pallas as pl
from jax.experimental.pallas import tpu as pltpu
from jax.sharding import PartitionSpec as P

L1_DEV = 4
PRIOR = 8.0
PLANE = 4
LANES = 128
MESH = pl.DeviceIdType.MESH


def split_counts(count, rows):
    high = count.astype(jnp.bfloat16).astype(jnp.float32)
    lane = lax.broadcasted_iota(jnp.int32, (rows, LANES), 1)
    return jnp.where(lane < LANES // 2, high, count - high)


def joined_counts(tail):
    return tail[:, :1] + tail[:, LANES // 2:LANES // 2 + 1]


def kernel(planes, rows_chunk, cols_chunk,
           emb_hbm, level_ref, cen_ref, empty_ref, reseed_ref,
           out_ref, count_ref,
           emb, cent, weights, lane_counts, parts, from_twin, to_mate, from_mate, to_plane, from_plane, own,
           emb_sem, z_send, z_recv, y_send, y_recv, t_send, t_recv, u_send, u_recv,
           rt_send, rt_recv, ry_send, ry_recv, rz_send, rz_recv):
    group = lax.axis_index("groups")
    me = lax.axis_index("owners")
    plane, lane = me // PLANE, me % PLANE
    y, c = lane // 2, lane % 2
    twin = plane * PLANE + y * 2 + (1 - c)
    mate = plane * PLANE + (1 - y) * 2 + c
    local, width = cen_ref.shape
    row_count = emb.shape[0]
    sub = local // L1_DEV
    block = PLANE * local
    wide = width + LANES

    def plane_mate(steps):
        return ((plane + steps) % planes) * PLANE + lane

    load = pltpu.make_async_copy(emb_hbm, emb, emb_sem)
    load.start()

    barrier = pltpu.get_barrier_semaphore()

    def greet(other):
        pl.semaphore_signal(barrier, inc=1, device_id=(group, other), device_id_type=MESH)

    greet(twin)
    greet(mate)
    for step in range(1, planes):
        greet(plane_mate(step))
    cent[0, c, y] = cen_ref[...].astype(jnp.bfloat16)
    pl.semaphore_wait(barrier, planes + 1)

    def remote(src, dst, send, recv, other):
        return pltpu.make_async_remote_copy(
            src_ref=src, dst_ref=dst, send_sem=send, recv_sem=recv,
            device_id=(group, other), device_id_type=MESH)

    def z_copy(s):
        return remote(cent.at[0, c, y], cent.at[s, c, y], z_send.at[s], z_recv.at[s], plane_mate(planes - s))

    def y_copy(s):
        return remote(cent.at[s, c, y], cent.at[s, c, y], y_send.at[s], y_recv.at[s], mate)

    def t_copy(s):
        return remote(cent.at[s, c, y], cent.at[s, c, y], t_send.at[s], t_recv.at[s], twin)

    def u_copy(s):
        return remote(cent.at[s, c, 1 - y], cent.at[s, c, 1 - y], u_send.at[s], u_recv.at[s], twin)

    def rt_copy(s):
        return remote(parts.at[s, 1 - c], from_twin.at[s], rt_send.at[s], rt_recv.at[s], twin)

    def ry_copy(s):
        return remote(to_mate.at[s], from_mate.at[s], ry_send.at[s], ry_recv.at[s], mate)

    def rz_copy(s):
        return remote(to_plane.at[s], from_plane.at[s], rz_send.at[s], rz_recv.at[s], plane_mate(s))

    y_copy(0).start()
    t_copy(0).start()
    for step in range(1, planes):
        z_copy(step).start()

    def spread_first(s):
        z_copy(s).wait_recv()
        y_copy(s).start()
        t_copy(s).start()

    def spread_second(s):
        y_copy(s).wait_recv()
        u_copy(s).start()

    def arrived(s):
        t_copy(s).wait_recv()
        u_copy(s).wait_recv()

    def replaced(first, rows, ids):
        hit = ids == empty_ref[...]
        row = jnp.sum(jnp.where(hit, reseed_ref[...] - me * row_count, 0), axis=1, keepdims=True)
        return jnp.sum(jnp.where(hit, 1, 0), axis=1, keepdims=True) > 0, row

    def weigh(s):
        target = (plane + s) % planes
        centroid = cent[s].reshape(block, width)
        as_f32 = centroid.astype(jnp.float32)
        half_norm = 0.5 * jnp.sum(as_f32 * as_f32, axis=1, keepdims=True)
        place = lax.broadcasted_iota(jnp.int32, (block, 1), 0)
        of_c, of_y, of_l = place // (2 * local), (place // local) % 2, place % local
        ids = target * block + (of_y * 2 + of_c) * local + of_l
        reseeded, source_row = replaced(0, block, ids)
        lane_counts[...] = jnp.zeros_like(lane_counts)

        @pl.loop(0, row_count // rows_chunk)
        def _(i):
            at = pl.ds(pl.multiple_of(i * rows_chunk, rows_chunk), rows_chunk)
            scores = lax.dot_general(
                cent[s].reshape(block, width), emb[at, :], (((1,), (1,)), ((), ())),
                preferred_element_type=jnp.float32)
            logits = (scores - half_norm) * (1.0 / math.sqrt(width))
            cluster = level_ref[:, at] - target * (PLANE * L1_DEV)
            picked = jnp.zeros((sub, rows_chunk), jnp.float32)
            order = []
            for g in range(PLANE * L1_DEV):
                gc, gy, gk = g // (2 * L1_DEV), (g // L1_DEV) % 2, g % L1_DEV
                order.append((gy * 2 + gc) * L1_DEV + gk)
            masks = [cluster == value for value in order]
            for g, mask in enumerate(masks):
                picked = jnp.where(mask, logits[g * sub:(g + 1) * sub], picked)
            raised = jnp.exp(picked - jnp.max(picked, axis=0, keepdims=True))
            soft = raised / jnp.sum(raised, axis=0, keepdims=True)
            spread = jnp.concatenate([jnp.where(mask, soft, 0.0) for mask in masks], axis=0)
            tally = lane_counts[...]
            for k in range(rows_chunk // LANES):
                tally = tally + spread[:, k * LANES:(k + 1) * LANES]
            lane_counts[...] = tally
            row = lax.broadcasted_iota(jnp.int32, (1, rows_chunk), 1) + i * rows_chunk
            chosen = jnp.where(row == source_row, 1.0, 0.0)
            weights[:, at] = jnp.where(reseeded, chosen, spread).astype(jnp.bfloat16)

    def collect(s):
        count = jnp.sum(lane_counts[...], axis=1, keepdims=True)
        parts[s, :, :, :, width:] = split_counts(count, block).astype(jnp.bfloat16).reshape(2, 2, local, LANES)

        @pl.loop(0, width // cols_chunk)
        def _(i):
            at = pl.ds(pl.multiple_of(i * cols_chunk, cols_chunk), cols_chunk)
            total = jnp.dot(weights[...], emb[:, at], preferred_element_type=jnp.float32)
            parts[s, :, :, :, at] = total.astype(jnp.bfloat16).reshape(2, 2, local, cols_chunk)

    def put(ref, s, value):
        tail = value[:, width:]
        ref[s, :, :width] = value[:, :width].astype(jnp.bfloat16)
        ref[s, :, width:] = split_counts(joined_counts(tail), local).astype(jnp.bfloat16)

    def reduce_second(s):
        rt_copy(s).wait_recv()
        value = parts[s, c, 1 - y].astype(jnp.float32) + from_twin[s, 1 - y].astype(jnp.float32)
        put(to_mate, s, value)
        ry_copy(s).start()

    def reduce_third(s):
        ry_copy(s).wait_recv()
        value = (parts[s, c, y].astype(jnp.float32) + from_twin[s, y].astype(jnp.float32)
                 + from_mate[s].astype(jnp.float32))

        @pl.when(s == 0)
        def _():
            own[...] = value

        @pl.when(s > 0)
        def _():
            put(to_plane, s, value)
            rz_copy(s).start()

    spread_second(0)
    spread_first(1)
    load.wait()

    @pl.loop(0, planes)
    def _(s):
        arrived(s)
        weigh(s)

        @pl.when(s >= 1)
        def _():
            reduce_second(s - 1)

        @pl.when(s + 1 < planes)
        def _():
            spread_second(s + 1)

        @pl.when(s + 2 < planes)
        def _():
            spread_first(s + 2)

        collect(s)
        rt_copy(s).start()

        @pl.when(s >= 1)
        def _():
            reduce_third(s - 1)

    reduce_second(planes - 1)
    reduce_third(planes - 1)

    total = own[...]
    for step in range(1, planes):
        rz_copy(step).wait_recv()
        total = total + from_plane[step].astype(jnp.float32)
    count = joined_counts(total[:, width:])
    ids = me * local + lax.broadcasted_iota(jnp.int32, (local, 1), 0)
    reseeded, _ = replaced(0, local, ids)
    sums = total[:, :width]
    updated = (sums + PRIOR * cen_ref[...]) / (count + PRIOR)
    out_ref[...] = jnp.where(reseeded, sums, updated)
    diagonal = (lax.broadcasted_iota(jnp.int32, (local, local), 0)
                == lax.broadcasted_iota(jnp.int32, (local, local), 1))
    count_ref[...] = jnp.sum(jnp.where(diagonal, count, 0.0), axis=0, keepdims=True)

    @pl.loop(0, planes)
    def _(s):
        y_copy(s).wait_send()
        t_copy(s).wait_send()
        u_copy(s).wait_send()
        rt_copy(s).wait_send()
        ry_copy(s).wait_send()

        @pl.when(s > 0)
        def _():
            z_copy(s).wait_send()
            rz_copy(s).wait_send()


def shards(owners, embeddings, level_ids, centroids, empty_ids, reseed_rows):
    row_count, width = embeddings.shape
    local = centroids.shape[0]
    planes = owners // PLANE
    wide = width + LANES
    block = PLANE * local
    bf16, f32 = jnp.bfloat16, jnp.float32
    vmem = pl.BlockSpec(memory_space=pltpu.VMEM)
    sem = pltpu.SemaphoreType.DMA((planes,))
    new_centroids, counts = pl.pallas_call(
        functools.partial(kernel, planes, 512, 512),
        out_shape=(jax.ShapeDtypeStruct((local, width), f32), jax.ShapeDtypeStruct((1, local), f32)),
        in_specs=[pl.BlockSpec(memory_space=pl.ANY), vmem, vmem, vmem, vmem],
        out_specs=(vmem, vmem),
        scratch_shapes=[
            pltpu.VMEM((row_count, width), bf16),
            pltpu.VMEM((planes, 2, 2, local, width), bf16),
            pltpu.VMEM((block, row_count), bf16),
            pltpu.VMEM((block, LANES), f32),
            pltpu.VMEM((planes, 2, 2, local, wide), bf16),
            pltpu.VMEM((planes, 2, local, wide), bf16),
            pltpu.VMEM((planes, local, wide), bf16),
            pltpu.VMEM((planes, local, wide), bf16),
            pltpu.VMEM((planes, local, wide), bf16),
            pltpu.VMEM((planes, local, wide), bf16),
            pltpu.VMEM((local, wide), f32),
            pltpu.SemaphoreType.DMA,
        ] + [sem] * 14,
        compiler_params=pltpu.CompilerParams(
            collective_id=0, has_side_effects=True, vmem_limit_bytes=48 * 1024 * 1024),
        cost_estimate=pl.CostEstimate(
            flops=4 * row_count * width * owners * local, transcendentals=row_count * 64,
            bytes_accessed=2 * row_count * width),
    )(embeddings, level_ids.reshape(1, -1), centroids, empty_ids.reshape(1, -1), reseed_rows.reshape(1, -1))
    return new_centroids, counts.reshape(-1)


def solution(mesh):
    in_specs = (
        P(("groups", "owners"), None),
        P(("groups", "owners")),
        P(("groups", "owners"), None),
        P("groups"),
        P("groups"),
    )
    out_specs = (P(("groups", "owners"), None), P(("groups", "owners")))
    return jax.shard_map(functools.partial(shards, mesh.shape["owners"]), mesh=mesh,
                         in_specs=in_specs, out_specs=out_specs, check_vma=False)
```

time: 197 us -> 72.2 us (0.37)
  blocking collectives: 91 us -> 0 us
  Pallas kernels: 0 us -> 67.1 us
  waiting for transfers between devices: 49.8 us -> 0 us
  matrix products: 22 us -> 0 us
  between operations: 14.9 us -> 0.65 us
  other arithmetic: 13.8 us -> 0 us
    pallas_call x0 -> x1, Pallas kernels: none -> 67.1 us  [shards(): pl.pallas_call(functools.partial(kernel, planes, 512, 512), out_shape=(ja...]
    psum x1 -> x0, blocking collectives: 61.2 us -> none  [shards(): lax.psum(picked.astype(jnp.bfloat16), 'owners').astype(jnp.float32)]
    all_gather x1 -> x0, waiting for transfers between devices: 49.8 us -> none  [shards(): every_centroid = lax.all_gather(centroid_b, 'owners', axis=0, tiled=True)]
    unnamed x1 -> x0, blocking collectives: 29.8 us -> none
    dot_general x3 -> x0, matrix products: 22 us -> none  [the longest x1 10.2 us: weigh(): lax.dot_general(centroid_b, row_block, (((1,), (1,)), ((), ())), preferre...]
    reduce_sum x4 -> x0, other arithmetic: 11.4 us -> none  [the longest x1 5.66 us: weigh(): counts = jnp.sum(weights, axis=1)]
    gather x1 -> x0, local copies, waits for them, and re-layouts: 4.27 us -> none  [shards(): embeddings[jnp.clip(local_pick, 0, row_count - 1)].astype(jnp.float32)]
    unnamed x17 -> x10, local copies, waits for them, and re-layouts: 0.75 us -> 4.25 us
  transfers between devices with their start and end apart: 2 -> 0, of which waited for: 1 -> 0; matrix products, arithmetic and copies ran while one was open for 6% -> 0% of each run, Pallas kernels for 0% -> 0%
where the time goes in v1:
time: 72.2 us; the launch traced here: 72 us
  Pallas kernels  67.1 us (93%)
  local copies, waits for them, and re-layouts  4.25 us (6%)
    pallas_call x1, Pallas kernels, shards(): pl.pallas_call(functools.partial(kernel, planes, 512, 512), out_shape=(ja...  67.1 us
    unnamed x10, local copies, waits for them, and re-layouts  4.25 us

profile of v1, /device:TPU:0, one launch (start us, length us, event | category | flops | bytes accessed | tf_op | source)
XLA Modules:
  0.0 72.0 jit_solution(11049883703110576459)
XLA Ops:
  0.6 0.0 copy-start
  0.6 1.0 %copy-done = f32[64,1536]{1,0:T(8,128)S(1)} copy-done((f32[64,1536]{1,0:T(8,128)S(1)}, f32[64,1536]{1,0:T(8,128)}, u32[]{:S(2)}) %copy-start) | copy-done | bytes 393240
  1.6 0.0 copy-start.1
  1.6 0.7 copy-done.1
  2.3 0.0 copy-start.2
  2.3 0.7 copy-done.2
  3.0 0.0 copy-start.3
  3.0 0.7 copy-done.3
  3.6 67.1 %shard_map.68 = (f32[64,1536]{1,0:T(8,128)S(1)}, f32[1,64]{1,0:T(1,128)S(1)}) custom-call(bf16[2048,1536]{1,0:T(8,128)(2,1)} %emb_hbm.1, s32[1,2048]{1,0:T(1,128)S(1)} %bitcast.4, f32[64,1536]{1,0:T(8,128)S(1)} %copy-done, s32[1,16]{1,0:T(1,128)S(1)} %bitcast.5, s32[1,16]{1,0:T(1,128)S(1)} %bitcast.6), custom_call_target="tpu_custom_call" | custom-call | flops 12884901888 | bytes 6291456 | tf_op jit(solution)/shard_map/pallas_call | solution.py:254
  70.7 0.7 %copy.9 = f32[64,1536]{1,0:T(8,128)} copy(f32[64,1536]{1,0:T(8,128)S(1)} %get-tuple-element.8) | data formatting | bytes 786432
  71.5 0.5 copy.10
Async XLA Ops:
  0.6 1.0 %copy-start = (f32[64,1536]{1,0:T(8,128)S(1)}, f32[64,1536]{1,0:T(8,128)}, u32[]{:S(2)}) copy-start(f32[64,1536]{1,0:T(8,128)} %cen_ref.1) | copy-start | bytes 1179652
  1.6 0.7 copy-start.1
  2.3 0.7 copy-start.2
  3.0 0.7 copy-start.3

commit v2 on v1

--- a/solution.py
+++ b/solution.py
@@ -26,10 +26,11 @@
 
 
 def kernel(planes, rows_chunk, cols_chunk,
-           emb_hbm, level_ref, cen_ref, empty_ref, reseed_ref,
+           emb_hbm, level_hbm, cen_hbm, empty_hbm, reseed_hbm,
            out_ref, count_ref,
-           emb, cent, weights, lane_counts, parts, from_twin, to_mate, from_mate, to_plane, from_plane, own,
-           emb_sem, z_send, z_recv, y_send, y_recv, t_send, t_recv, u_send, u_recv,
+           emb, level_ref, cen_ref, empty_ref, reseed_ref,
+           cent, weights, lane_counts, parts, from_twin, to_mate, from_mate, to_plane, from_plane, own,
+           load_sem, z_send, z_recv, y_send, y_recv, t_send, t_recv, u_send, u_recv,
            rt_send, rt_recv, ry_send, ry_recv, rz_send, rz_recv):
     group = lax.axis_index("groups")
     me = lax.axis_index("owners")
@@ -41,13 +42,15 @@
     row_count = emb.shape[0]
     sub = local // L1_DEV
     block = PLANE * local
-    wide = width + LANES
-
-    def plane_mate(steps):
-        return ((plane + steps) % planes) * PLANE + lane
-
-    load = pltpu.make_async_copy(emb_hbm, emb, emb_sem)
-    load.start()
+
+    def plane_mate(p):
+        return p * PLANE + lane
+
+    loads = [pltpu.make_async_copy(src, dst, load_sem.at[i]) for i, (src, dst) in enumerate([
+        (cen_hbm, cen_ref), (level_hbm, level_ref), (empty_hbm, empty_ref), (reseed_hbm, reseed_ref),
+        (emb_hbm, emb)])]
+    for load in loads:
+        load.start()
 
     barrier = pltpu.get_barrier_semaphore()
 
@@ -57,68 +60,100 @@
     greet(twin)
     greet(mate)
     for step in range(1, planes):
-        greet(plane_mate(step))
-    cent[0, c, y] = cen_ref[...].astype(jnp.bfloat16)
+        greet(plane_mate((plane + step) % planes))
+    loads[0].wait()
+    cent[plane, c, y] = cen_ref[...].astype(jnp.bfloat16)
     pl.semaphore_wait(barrier, planes + 1)
+
+    both = jnp.minimum(plane, planes - 1 - plane)
+
+    def nth(i):
+        near = jnp.where(i % 2 == 1, plane + (i + 1) // 2, plane - i // 2)
+        far = jnp.where(plane < planes - 1 - plane, plane + i - both, plane - i + both)
+        return jnp.where(i <= 2 * both, near, far)
 
     def remote(src, dst, send, recv, other):
         return pltpu.make_async_remote_copy(
             src_ref=src, dst_ref=dst, send_sem=send, recv_sem=recv,
             device_id=(group, other), device_id_type=MESH)
 
-    def z_copy(s):
-        return remote(cent.at[0, c, y], cent.at[s, c, y], z_send.at[s], z_recv.at[s], plane_mate(planes - s))
-
-    def y_copy(s):
-        return remote(cent.at[s, c, y], cent.at[s, c, y], y_send.at[s], y_recv.at[s], mate)
-
-    def t_copy(s):
-        return remote(cent.at[s, c, y], cent.at[s, c, y], t_send.at[s], t_recv.at[s], twin)
-
-    def u_copy(s):
-        return remote(cent.at[s, c, 1 - y], cent.at[s, c, 1 - y], u_send.at[s], u_recv.at[s], twin)
-
-    def rt_copy(s):
-        return remote(parts.at[s, 1 - c], from_twin.at[s], rt_send.at[s], rt_recv.at[s], twin)
-
-    def ry_copy(s):
-        return remote(to_mate.at[s], from_mate.at[s], ry_send.at[s], ry_recv.at[s], mate)
-
-    def rz_copy(s):
-        return remote(to_plane.at[s], from_plane.at[s], rz_send.at[s], rz_recv.at[s], plane_mate(s))
-
-    y_copy(0).start()
-    t_copy(0).start()
-    for step in range(1, planes):
-        z_copy(step).start()
-
-    def spread_first(s):
-        z_copy(s).wait_recv()
-        y_copy(s).start()
-        t_copy(s).start()
-
-    def spread_second(s):
-        y_copy(s).wait_recv()
-        u_copy(s).start()
-
-    def arrived(s):
-        t_copy(s).wait_recv()
-        u_copy(s).wait_recv()
-
-    def replaced(first, rows, ids):
+    def up_copy(p):
+        return remote(cent.at[p, c, y], cent.at[p, c, y], z_send.at[p, 0], z_recv.at[p], plane_mate(plane + 1))
+
+    def down_copy(p):
+        return remote(cent.at[p, c, y], cent.at[p, c, y], z_send.at[p, 1], z_recv.at[p], plane_mate(plane - 1))
+
+    def y_copy(p):
+        return remote(cent.at[p, c, y], cent.at[p, c, y], y_send.at[p], y_recv.at[p], mate)
+
+    def t_copy(p):
+        return remote(cent.at[p, c, y], cent.at[p, c, y], t_send.at[p], t_recv.at[p], twin)
+
+    def u_copy(p):
+        return remote(cent.at[p, c, 1 - y], cent.at[p, c, 1 - y], u_send.at[p], u_recv.at[p], twin)
+
+    def rt_copy(p):
+        return remote(parts.at[p, 1 - c], from_twin.at[p], rt_send.at[p], rt_recv.at[p], twin)
+
+    def ry_copy(p):
+        return remote(to_mate.at[p], from_mate.at[p], ry_send.at[p], ry_recv.at[p], mate)
+
+    def rz_copy(p):
+        return remote(to_plane.at[p], from_plane.at[plane], rz_send.at[p], rz_recv.at[plane], plane_mate(p))
+
+    def rz_arrival(p):
+        return remote(to_plane.at[p], from_plane.at[p], rz_send.at[p], rz_recv.at[p], plane_mate(p))
+
+    def relay(p):
+        @pl.when((p <= plane) & (plane < planes - 1))
+        def _():
+            up_copy(p).start()
+
+        @pl.when((p >= plane) & (plane > 0))
+        def _():
+            down_copy(p).start()
+
+    def relay_sent(p):
+        @pl.when((p <= plane) & (plane < planes - 1))
+        def _():
+            up_copy(p).wait_send()
+
+        @pl.when((p >= plane) & (plane > 0))
+        def _():
+            down_copy(p).wait_send()
+
+    y_copy(plane).start()
+    relay(plane)
+    t_copy(plane).start()
+
+    def spread_first(p):
+        up_copy(p).wait_recv()
+        relay(p)
+        y_copy(p).start()
+        t_copy(p).start()
+
+    def spread_second(p):
+        y_copy(p).wait_recv()
+        u_copy(p).start()
+
+    def arrived(p):
+        t_copy(p).wait_recv()
+        u_copy(p).wait_recv()
+
+    def replaced(ids):
         hit = ids == empty_ref[...]
         row = jnp.sum(jnp.where(hit, reseed_ref[...] - me * row_count, 0), axis=1, keepdims=True)
         return jnp.sum(jnp.where(hit, 1, 0), axis=1, keepdims=True) > 0, row
 
     def weigh(s):
-        target = (plane + s) % planes
+        target = s
         centroid = cent[s].reshape(block, width)
         as_f32 = centroid.astype(jnp.float32)
         half_norm = 0.5 * jnp.sum(as_f32 * as_f32, axis=1, keepdims=True)
         place = lax.broadcasted_iota(jnp.int32, (block, 1), 0)
         of_c, of_y, of_l = place // (2 * local), (place // local) % 2, place % local
         ids = target * block + (of_y * 2 + of_c) * local + of_l
-        reseeded, source_row = replaced(0, block, ids)
+        reseeded, source_row = replaced(ids)
         lane_counts[...] = jnp.zeros_like(lane_counts)
 
         @pl.loop(0, row_count // rows_chunk)
@@ -174,53 +209,64 @@
         value = (parts[s, c, y].astype(jnp.float32) + from_twin[s, y].astype(jnp.float32)
                  + from_mate[s].astype(jnp.float32))
 
-        @pl.when(s == 0)
+        @pl.when(s == plane)
         def _():
             own[...] = value
 
-        @pl.when(s > 0)
+        @pl.when(s != plane)
         def _():
             put(to_plane, s, value)
             rz_copy(s).start()
 
-    spread_second(0)
-    spread_first(1)
-    load.wait()
+    last = planes - 1
+
+    def turn(k):
+        return nth(jnp.where(k == last, 0, k + 1))
+
+    spread_first(nth(1))
+    spread_second(plane)
+    spread_first(nth(2))
+    spread_second(nth(1))
+    for load in loads[1:]:
+        load.wait()
 
     @pl.loop(0, planes)
-    def _(s):
-        arrived(s)
-        weigh(s)
-
-        @pl.when(s >= 1)
-        def _():
-            reduce_second(s - 1)
-
-        @pl.when(s + 1 < planes)
-        def _():
-            spread_second(s + 1)
-
-        @pl.when(s + 2 < planes)
-        def _():
-            spread_first(s + 2)
-
-        collect(s)
-        rt_copy(s).start()
-
-        @pl.when(s >= 1)
-        def _():
-            reduce_third(s - 1)
-
-    reduce_second(planes - 1)
-    reduce_third(planes - 1)
+    def _(k):
+        p = turn(k)
+        arrived(p)
+        weigh(p)
+
+        @pl.when(k >= 2)
+        def _():
+            reduce_third(turn(k - 2))
+
+        @pl.when(k >= 1)
+        def _():
+            reduce_second(turn(k - 1))
+
+        @pl.when(k + 3 <= last)
+        def _():
+            spread_first(nth(k + 3))
+
+        @pl.when(k + 2 <= last)
+        def _():
+            spread_second(nth(k + 2))
+
+        collect(p)
+        rt_copy(p).start()
+
+    reduce_second(plane)
+    reduce_third(turn(last - 1))
+    reduce_third(plane)
 
     total = own[...]
     for step in range(1, planes):
-        rz_copy(step).wait_recv()
-        total = total + from_plane[step].astype(jnp.float32)
+        p = nth(step)
+        rz_arrival(p).wait_recv()
+        total = total + from_plane[p].astype(jnp.float32)
     count = joined_counts(total[:, width:])
     ids = me * local + lax.broadcasted_iota(jnp.int32, (local, 1), 0)
-    reseeded, _ = replaced(0, local, ids)
+    reseeded, _ = replaced(ids)
     sums = total[:, :width]
     updated = (sums + PRIOR * cen_ref[...]) / (count + PRIOR)
     out_ref[...] = jnp.where(reseeded, sums, updated)
@@ -229,17 +275,17 @@
     count_ref[...] = jnp.sum(jnp.where(diagonal, count, 0.0), axis=0, keepdims=True)
 
     @pl.loop(0, planes)
-    def _(s):
-        y_copy(s).wait_send()
-        t_copy(s).wait_send()
-        u_copy(s).wait_send()
-        rt_copy(s).wait_send()
-        ry_copy(s).wait_send()
-
-        @pl.when(s > 0)
-        def _():
-            z_copy(s).wait_send()
-            rz_copy(s).wait_send()
+    def _(p):
+        y_copy(p).wait_send()
+        t_copy(p).wait_send()
+        u_copy(p).wait_send()
+        relay_sent(p)
+        rt_copy(p).wait_send()
+        ry_copy(p).wait_send()
+
+        @pl.when(p != plane)
+        def _():
+            rz_copy(p).wait_send()
 
 
 def shards(owners, embeddings, level_ids, centroids, empty_ids, reseed_rows):
@@ -254,10 +300,14 @@
     new_centroids, counts = pl.pallas_call(
         functools.partial(kernel, planes, 512, 512),
         out_shape=(jax.ShapeDtypeStruct((local, width), f32), jax.ShapeDtypeStruct((1, local), f32)),
-        in_specs=[pl.BlockSpec(memory_space=pl.ANY), vmem, vmem, vmem, vmem],
+        in_specs=[pl.BlockSpec(memory_space=pl.ANY)] * 5,
         out_specs=(vmem, vmem),
         scratch_shapes=[
             pltpu.VMEM((row_count, width), bf16),
+            pltpu.VMEM((1, row_count), jnp.int32),
+            pltpu.VMEM((local, width), f32),
+            pltpu.VMEM((1, empty_ids.shape[0]), jnp.int32),
+            pltpu.VMEM((1, empty_ids.shape[0]), jnp.int32),
             pltpu.VMEM((planes, 2, 2, local, width), bf16),
             pltpu.VMEM((block, row_count), bf16),
             pltpu.VMEM((block, LANES), f32),
@@ -268,10 +318,11 @@
             pltpu.VMEM((planes, local, wide), bf16),
             pltpu.VMEM((planes, local, wide), bf16),
             pltpu.VMEM((local, wide), f32),
-            pltpu.SemaphoreType.DMA,
-        ] + [sem] * 14,
+            pltpu.SemaphoreType.DMA((5,)),
+            pltpu.SemaphoreType.DMA((planes, 2)),
+        ] + [sem] * 13,
         compiler_params=pltpu.CompilerParams(
-            collective_id=0, has_side_effects=True, vmem_limit_bytes=48 * 1024 * 1024),
+            collective_id=0, has_side_effects=True, vmem_limit_bytes=60 * 1024 * 1024),
         cost_estimate=pl.CostEstimate(
             flops=4 * row_count * width * owners * local, transcendentals=row_count * 64,
             bytes_accessed=2 * row_count * width),

time: 72.2 us -> 68.8 us (0.953)
  Pallas kernels: 67.1 us -> 65.1 us
  local copies, waits for them, and re-layouts: 4.25 us -> 2.89 us
    pallas_call x1, Pallas kernels: 67.1 us -> 65.1 us  [shards(): pl.pallas_call(functools.partial(kernel, planes, 512, 512), out_shape=(ja...]
    unnamed x10 -> x2, local copies, waits for them, and re-layouts: 4.25 us -> 2.89 us
where the time goes in v2:
time: 68.8 us; the launch traced here: 68.6 us
  Pallas kernels  65.1 us (95%)
  local copies, waits for them, and re-layouts  2.89 us (4%)
    pallas_call x1, Pallas kernels, shards(): pl.pallas_call(functools.partial(kernel, planes, 512, 512), out_shape=(ja...  65.1 us
    unnamed x2, local copies, waits for them, and re-layouts  2.89 us

profile of v2, /device:TPU:0, one launch (start us, length us, event | category | flops | bytes accessed | tf_op | source)
XLA Modules:
  0.0 68.6 jit_solution(251910246748039890)
XLA Ops:
  0.6 65.1 %shard_map.68 = (f32[64,1536]{1,0:T(8,128)}, f32[1,64]{1,0:T(1,128)}) custom-call(bf16[2048,1536]{1,0:T(8,128)(2,1)} %emb_hbm.1, s32[1,2048]{1,0:T(1,128)} %bitcast.4, f32[64,1536]{1,0:T(8,128)} %cen_hbm.1, s32[1,16]{1,0:T(1,128)} %bitcast.5, s32[1,16]{1,0:T(1,128)} %bitcast.6), custom_call_target="tpu_custom_call" | custom-call | flops 12884901888 | bytes 6291456 | tf_op jit(solution)/shard_map/pallas_call | solution.py:300
  65.7 1.8 %copy.9 = f32[64,1536]{1,0:T(8,128)} copy(f32[64,1536]{1,0:T(8,128)} %get-tuple-element.8) | data formatting | bytes 786432
  67.5 1.1 %copy.10 = f32[64]{0:T(128)} copy(f32[64]{0:T(128)} %bitcast.7) | data formatting | bytes 512

commit v3 on v2

--- a/solution.py
+++ b/solution.py
@@ -221,12 +221,10 @@
     last = planes - 1
 
     def turn(k):
-        return nth(jnp.where(k == last, 0, k + 1))
-
+        return nth(jnp.where(k == 0, 0, jnp.where(k == last, 1, k + 1)))
+
+    spread_second(plane)
     spread_first(nth(1))
-    spread_second(plane)
-    spread_first(nth(2))
-    spread_second(nth(1))
     for load in loads[1:]:
         load.wait()
 
@@ -244,20 +242,31 @@
         def _():
             reduce_second(turn(k - 1))
 
-        @pl.when(k + 3 <= last)
+        @pl.when(k == 0)
+        def _():
+            spread_second(nth(1))
+            spread_first(nth(2))
+
+        @pl.when((k >= 1) & (k + 2 <= last))
+        def _():
+            spread_second(nth(k + 2))
+
+        @pl.when((k >= 1) & (k + 3 <= last))
         def _():
             spread_first(nth(k + 3))
-
-        @pl.when(k + 2 <= last)
-        def _():
-            spread_second(nth(k + 2))
 
         collect(p)
         rt_copy(p).start()
 
-    reduce_second(plane)
+        @pl.when(k == 0)
+        def _():
+            spread_second(nth(2))
+            spread_first(nth(3))
+
+
+    reduce_second(turn(last))
     reduce_third(turn(last - 1))
-    reduce_third(plane)
+    reduce_third(turn(last))
 
     total = own[...]
     for step in range(1, planes):
@@ -298,7 +307,7 @@
     vmem = pl.BlockSpec(memory_space=pltpu.VMEM)
     sem = pltpu.SemaphoreType.DMA((planes,))
     new_centroids, counts = pl.pallas_call(
-        functools.partial(kernel, planes, 512, 512),
+        functools.partial(kernel, planes, row_count, width),
         out_shape=(jax.ShapeDtypeStruct((local, width), f32), jax.ShapeDtypeStruct((1, local), f32)),
         in_specs=[pl.BlockSpec(memory_space=pl.ANY)] * 5,
         out_specs=(vmem, vmem),

time: 68.8 us -> 66.4 us (0.965)
  the two profiles are of different devices: /device:TPU:0 before, /device:TPU:23 now
where the time goes in v3:
time: 66.4 us; the launch traced here: 66.2 us
  Pallas kernels  62.7 us (94%)
  local copies, waits for them, and re-layouts  2.89 us (4%)
    pallas_call x1, Pallas kernels, shards(): pl.pallas_call(functools.partial(kernel, planes, row_count, width), out_s...  62.7 us
    unnamed x2, local copies, waits for them, and re-layouts  2.89 us

profile of v3, /device:TPU:23, one launch (start us, length us, event | category | flops | bytes accessed | tf_op | source)
XLA Modules:
  0.0 66.2 jit_solution(16567171472674398879)
XLA Ops:
  0.6 62.7 %shard_map.68 = (f32[64,1536]{1,0:T(8,128)}, f32[1,64]{1,0:T(1,128)}) custom-call(bf16[2048,1536]{1,0:T(8,128)(2,1)} %emb_hbm.1, s32[1,2048]{1,0:T(1,128)} %bitcast.4, f32[64,1536]{1,0:T(8,128)} %cen_hbm.1, s32[1,16]{1,0:T(1,128)} %bitcast.5, s32[1,16]{1,0:T(1,128)} %bitcast.6), custom_call_target="tpu_custom_call" | custom-call | flops 12884901888 | bytes 6291456 | tf_op jit(solution)/shard_map/pallas_call | solution.py:309
  63.3 1.8 %copy.9 = f32[64,1536]{1,0:T(8,128)} copy(f32[64,1536]{1,0:T(8,128)} %get-tuple-element.8) | data formatting | bytes 786432
  65.1 1.1 %copy.10 = f32[64]{0:T(128)} copy(f32[64]{0:T(128)} %bitcast.7) | data formatting | bytes 512

commit v4 on v3

--- a/solution.py
+++ b/solution.py
@@ -234,10 +234,6 @@
         arrived(p)
         weigh(p)
 
-        @pl.when(k >= 2)
-        def _():
-            reduce_third(turn(k - 2))
-
         @pl.when(k >= 1)
         def _():
             reduce_second(turn(k - 1))
@@ -254,6 +250,10 @@
         @pl.when((k >= 1) & (k + 3 <= last))
         def _():
             spread_first(nth(k + 3))
+
+        @pl.when(k >= 2)
+        def _():
+            reduce_third(turn(k - 2))
 
         collect(p)
         rt_copy(p).start()

time: 66.4 us -> 65.7 us (0.989)
  the two profiles are of different devices: /device:TPU:23 before, /device:TPU:18 now
where the time goes in v4:
time: 65.7 us; the launch traced here: 65.5 us
  Pallas kernels  62 us (94%)
  local copies, waits for them, and re-layouts  2.89 us (4%)
    pallas_call x1, Pallas kernels, shards(): pl.pallas_call(functools.partial(kernel, planes, row_count, width), out_s...  62 us
    unnamed x2, local copies, waits for them, and re-layouts  2.89 us

profile of v4, /device:TPU:18, one launch (start us, length us, event | category | flops | bytes accessed | tf_op | source)
XLA Modules:
  0.0 65.5 jit_solution(16392363973041018106)
XLA Ops:
  0.6 62.0 %shard_map.68 = (f32[64,1536]{1,0:T(8,128)}, f32[1,64]{1,0:T(1,128)}) custom-call(bf16[2048,1536]{1,0:T(8,128)(2,1)} %emb_hbm.1, s32[1,2048]{1,0:T(1,128)} %bitcast.4, f32[64,1536]{1,0:T(8,128)} %cen_hbm.1, s32[1,16]{1,0:T(1,128)} %bitcast.5, s32[1,16]{1,0:T(1,128)} %bitcast.6), custom_call_target="tpu_custom_call" | custom-call | flops 12884901888 | bytes 6291456 | tf_op jit(solution)/shard_map/pallas_call | solution.py:309
  62.6 1.8 %copy.9 = f32[64,1536]{1,0:T(8,128)} copy(f32[64,1536]{1,0:T(8,128)} %get-tuple-element.8) | data formatting | bytes 786432
  64.4 1.1 %copy.10 = f32[64]{0:T(128)} copy(f32[64]{0:T(128)} %bitcast.7) | data formatting | bytes 512
